TPU v7x, 256 devices: a whole 4x4x8 slice. The times are simulated.
256 devices in a mesh: dp: 32 (over x, z), seq: 8 (over y, core).
Axes of the slice: x: 4, y: 4, z: 8, core: 2. Of those that a mesh axis runs over, the one named last changes fastest.
Arguments:
- pixels: bfloat16 [32768, 1176], P(('dp', 'seq')), may hold values from -6 to 6
- patch_weight: bfloat16 [1176, 1280], replicated, may hold values from -0.1875 to 0.1875
- ln_gain: float32 [1280], replicated, may hold values from 0.1 to 1.9
- ln_bias: float32 [1280], replicated, may hold values from -1.5 to 1.5
- qkv_weight: bfloat16 [1280, 3840], P('dp'), may hold values from -4 to 4
- qkv_bias: float32 [3840], replicated, may hold values from -2.5 to 2.5
- out_weight: bfloat16 [1280, 1280], P('dp'), may hold values from -0.15625 to 0.15625
- out_bias: float32 [1280], replicated, may hold values from -1.5 to 1.5
- offsets: int32 [32, 3], P('dp'), may hold values from 0 to 854, as said below
- widths: int32 [32, 3], P('dp'), may hold values from 16 to 64
Outputs:
- encoded: bfloat16 [32768, 1280], P(('dp', 'seq'))
Inputs may be any that keep to these rules, and one draw needn't show every extreme that they name: In every group the first offset is 0 and offsets rise; every image holds 170 or more tokens and the last image ends at position 1024; in some group the last image holds exactly 170 tokens.
All inputs are finite; a program needn't handle non-finite values.
Results may differ from a plain program's by a relative error of at most 0.012.
Values may be sent and summed in bfloat16 or wider, within the bound.
No kernel may reach another device: no remote copies, remote signals or barrier semaphores. Data moves between devices by JAX's collectives and lax.ppermute only.
A program may use at most 64 MiB of HBM per device.

v0:
```python
import jax
import jax.numpy as jnp
from jax import lax
from jax.sharding import PartitionSpec as P

HEADS = 16
HDIM = 80


def image_lookup(positions, starts):
    return jnp.sum((positions[:, None] >= starts[None, :]).astype(jnp.int32), axis=1) - 1


def rotation_tables(positions, starts, image_widths, head_size):
    image_index = image_lookup(positions, starts)
    onehot = (image_index[:, None] == jnp.arange(starts.shape[0], dtype=jnp.int32)[None, :]).astype(
        jnp.int32
    )
    first_position = jnp.sum(onehot * starts[None, :], axis=1)
    across = jnp.sum(onehot * image_widths[None, :], axis=1)
    within = positions - first_position
    row_index = within // across
    column_index = within - row_index * across
    quarter = head_size // 4
    inverse = 1.0 / 10000.0 ** (jnp.arange(quarter, dtype=jnp.float32) * 2.0 / (head_size // 2))
    angles = jnp.concatenate(
        [
            row_index.astype(jnp.float32)[:, None] * inverse[None, :],
            column_index.astype(jnp.float32)[:, None] * inverse[None, :],
        ],
        axis=1,
    )
    angles = jnp.concatenate([angles, angles], axis=1)
    return (jnp.cos(angles), jnp.sin(angles), image_index)


def rotate_heads(values, cosine, sine_table, head_size):
    half_size = head_size // 2
    turned = jnp.concatenate([-values[..., half_size:], values[..., :half_size]], axis=-1)
    return values * cosine[:, None, :] + turned * sine_table[:, None, :]


def layer_norm(embedded, ln_gain, ln_bias):
    values = embedded.astype(jnp.float32)
    center = values - jnp.mean(values, axis=-1, keepdims=True)
    variance = jnp.mean(center * center, axis=-1, keepdims=True)
    return (center * lax.rsqrt(variance + 1e-06) * ln_gain + ln_bias).astype(jnp.bfloat16)


def block_length(count):
    length = min(count, 512)
    while count % length:
        length -= 1
    return length


def attend_block(state, queries3, key_block, value_block, query_image, key_image, score_scale):
    running_max, running_total, accum = state
    count = key_block.shape[0]
    scores = (
        jnp.einsum(
            "qhd,khd->hqk",
            queries3,
            key_block.reshape(count, HEADS, HDIM),
            preferred_element_type=jnp.float32,
        )
        * score_scale
    )
    allowed = (query_image[:, None] == key_image[None, :])[None]
    scores = jnp.where(allowed, scores, -1e30)
    new_max = jnp.maximum(running_max, jnp.max(scores, axis=-1))
    weights = jnp.where(allowed, jnp.exp(scores - new_max[..., None]), 0.0)
    factor = jnp.exp(running_max - new_max)
    running_total = running_total * factor + jnp.sum(weights, axis=-1)
    part_sum = jnp.einsum(
        "hqk,khd->qhd",
        weights.astype(jnp.bfloat16),
        value_block.reshape(count, HEADS, HDIM),
        preferred_element_type=jnp.float32,
    )
    accum = accum * factor.T[:, :, None] + part_sum
    return (new_max, running_total, accum)


def per_device(
    pixels,
    patch_weight,
    ln_gain,
    ln_bias,
    qkv_weight,
    qkv_bias,
    out_weight,
    out_bias,
    offsets,
    widths,
):
    local_pixels = lax.all_to_all(pixels, "dp", split_axis=0, concat_axis=0, tiled=True)
    tok_rows = local_pixels.shape[0]
    dmodel = patch_weight.shape[1]
    score_scale = HDIM ** (-0.5)
    embedded = jnp.dot(local_pixels, patch_weight, preferred_element_type=jnp.float32).astype(
        jnp.bfloat16
    )
    normed = layer_norm(embedded, ln_gain, ln_bias)
    columns = normed
    projected = (
        jnp.dot(
            columns,
            lax.all_gather(qkv_weight, "dp", axis=0, tiled=True),
            preferred_element_type=jnp.float32,
        )
        + qkv_bias
    )
    starts = offsets[0]
    image_widths = widths[0]
    positions = lax.axis_index("seq") * tok_rows + jnp.arange(tok_rows, dtype=jnp.int32)
    cosine, sine_table, query_image = rotation_tables(positions, starts, image_widths, HDIM)
    queries = (
        rotate_heads(projected[:, :dmodel].reshape(tok_rows, HEADS, HDIM), cosine, sine_table, HDIM)
        .reshape(tok_rows, dmodel)
        .astype(jnp.bfloat16)
    )
    key_rows = (
        rotate_heads(
            projected[:, dmodel : 2 * dmodel].reshape(tok_rows, HEADS, HDIM),
            cosine,
            sine_table,
            HDIM,
        )
        .reshape(tok_rows, dmodel)
        .astype(jnp.bfloat16)
    )
    values = projected[:, 2 * dmodel :].astype(jnp.bfloat16)
    queries3 = queries.reshape(tok_rows, HEADS, HDIM)
    initial = (
        jnp.full((HEADS, tok_rows), -1e30, jnp.float32),
        jnp.zeros((HEADS, tok_rows), jnp.float32),
        jnp.zeros((tok_rows, HEADS, HDIM), jnp.float32),
    )
    piece_keys = lax.all_gather(key_rows, "seq", axis=0, tiled=True)
    piece_values = lax.all_gather(values, "seq", axis=0, tiled=True)
    count = piece_keys.shape[0]
    length = block_length(count)

    def one_block(block_index, inner):
        first_row = block_index * length
        key_block = lax.dynamic_slice_in_dim(piece_keys, first_row, length, 0)
        value_block = lax.dynamic_slice_in_dim(piece_values, first_row, length, 0)
        key_image = image_lookup(first_row + jnp.arange(length, dtype=jnp.int32), starts)
        return attend_block(
            inner, queries3, key_block, value_block, query_image, key_image, score_scale
        )

    final_state = lax.fori_loop(0, count // length, one_block, initial)
    attended = (
        (final_state[2] / final_state[1].T[:, :, None])
        .reshape(tok_rows, dmodel)
        .astype(jnp.bfloat16)
    )
    columns = attended
    mixed = jnp.dot(
        columns,
        lax.all_gather(out_weight, "dp", axis=0, tiled=True),
        preferred_element_type=jnp.float32,
    )
    return (embedded.astype(jnp.float32) + mixed + out_bias).astype(jnp.bfloat16)


def solution(mesh):
    in_specs = (
        P(("dp", "seq"), None),
        P(),
        P(),
        P(),
        P("dp", None),
        P(),
        P("dp", None),
        P(),
        P("dp", None),
        P("dp", None),
    )
    out_specs = P(("dp", "seq"), None)
    return jax.shard_map(
        per_device, mesh=mesh, in_specs=in_specs, out_specs=out_specs, check_vma=False
    )
```

profile of v0, /device:TPU:8, one launch (start us, length us, event | category | flops | bytes accessed | tf_op | source)
XLA Modules:
  0.0 290.6 jit_solution(15201041775588603741)
XLA Ops:
  7.3 1.3 copy.27
  9.4 11.4 %all-to-all-start = ((bf16[32,4,1176]{2,1,0:T(4,128)(2,1)}), bf16[32,4,1176]{2,1,0:T(4,128)(2,1)}, u32[]{:S(2)}, u32[]{:S(2)}) async-start(bf16[32,4,1176]{2,1,0:T(4,128)(2,1)} %all_to_all.8), calls=%async_computation | async-start | bytes 655360 | tf_op jit(solution)/shard_map/all_to_all | solution.py:97
  23.7 2.2 copy.28
  25.9 8.5 %all-to-all-done = bf16[32,4,1176]{2,1,0:T(4,128)(2,1)} async-done(((bf16[32,4,1176]{2,1,0:T(4,128)(2,1)}), bf16[32,4,1176]{2,1,0:T(4,128)(2,1)}, u32[]{:S(2)}, u32[]{:S(2)}) %all-to-all-start) | async-done | bytes 301088 | tf_op jit(solution)/shard_map/all_to_all | solution.py:97
  37.3 81.0 %all-gather.5.cloned.1.call-done = bf16[1280,3840]{1,0:T(8,128)(2,1)} async-done(((bf16[40,3840]{1,0:T(8,128)(2,1)}), bf16[1280,3840]{1,0:T(8,128)(2,1)}) %all-gather.5.cloned.1.call-update) | async-done | bytes 9830416 | tf_op jit(solution)/shard_map/all_gather | solution.py:109
  118.3 5.5 %convolution_add_fusion = f32[128,3840]{1,0:T(8,128)S(1)} fusion(bf16[1280,3840]{1,0:T(8,128)(2,1)} %all-gather.5.cloned.1.call-done, f32[3840]{0:T(1024)S(1)} %copy-done.7, f32[128,1280]{1,0:T(8,128)} %copy-done.2, f32[1280]{0:T(1024)S(1)} %copy-done.4, f32[1280]{0:T(1024)S(1)} %copy-done.5, f32[128]{0:T(128)S(1)} %add_rsqrt_fusion, ...), kind=kOutput, calls=%fused_computation.24 | convolution fusion | flops 1259601920 | bytes 12478464 | tf_op jit(solution)/shard_map/dot_general | solution.py:107
  123.8 1.3 copy-done.3
  126.3 2.1 copy.29
  128.4 2.2 copy.32
  130.6 1.4 slice_negate_fusion
  131.9 1.2 maximum_multiply_fusion.1
  133.1 2.2 copy.30
  135.2 2.2 copy.33
  137.4 2.9 add_convert_fusion
  140.4 1.8 slice.41
  142.8 1.2 copy.34
  144.0 21.3 %all-gather.7.cloned.1.call-done = bf16[1024,1280]{1,0:T(8,128)(2,1)} async-done(((bf16[128,1280]{1,0:T(8,128)(2,1)}), bf16[1024,1280]{1,0:T(8,128)(2,1)}) %all-gather.7.cloned.1.call-update) | async-done | bytes 2621456 | tf_op jit(solution)/shard_map/all_gather | solution.py:140
  165.3 31.1 %all-gather.9.cloned.1.call-done = bf16[1024,1280]{1,0:T(8,128)(2,1)} async-done(((bf16[128,1280]{1,0:T(8,128)(2,1)}), bf16[1024,1280]{1,0:T(8,128)(2,1)}) %all-gather.9.cloned.1.call-update) | async-done | bytes 2621456 | tf_op jit(solution)/shard_map/all_gather | solution.py:141
  196.5 37.7 %while.20 = (s32[]{:T(128)}, f32[16,128]{1,0:T(8,128)S(1)}, f32[16,128]{1,0:T(8,128)S(1)}, f32[128,16,80]{0,2,1:T(8,128)}, s32[128]{0:T(128)S(1)}, /*index=5*/s3...) while((s32[]{:T(128)}, f32[16,128]{1,0:T(8,128)S(1)}, ...), condition=%wide.region_9.10_spmd.clone, body=%wide.region_5.9_spmd.clone.sunk | while | flops 349750272 | bytes 44511972 | solution.py:154
  196.5 3.5 %constant_dynamic-slice_fusion.3 = (bf16[512,1280]{1,0:T(8,128)(2,1)}, bf16[512,1280]{1,0:T(8,128)(2,1)}) fusion(bf16[1024,1280]{1,0:T(8,128)(2,1)} %get-tuple-element.432, s32[]{:T(128)S(6)} %select_n.85, bf16[1024,1280]{1,0:T(8,128)(2,1)} %get-tuple-element.430), kind=kLoop, calls=%fused_computation.19.clone.1 | loop fusion | bytes 5242884 | tf_op jit(solution)/shard_map/while/body/eval_jaxpr/dynamic_slice | solution.py:148
  199.9 2.4 copy.42
  202.6 4.3 %fusion.50 = (f32[16,128]{1,0:T(8,128)S(1)}, f32[16,512,128]{2,1,0:T(8,128)}) fusion(pred[128,512]{0,1:T(8,128)(4,1)S(1)} %broadcast_compare_fusion.2, bf16[512,16,80]{0,2,1:T(8,128)(2,1)} %bitcast.64, bf16[128,16,80]{0,2,1:T(8,128)(2,1)S(1)} %get-tuple-element.431), kind=kOutput, calls=%fused_computation.2.clone.1 | convolution fusion | flops 170915840 | bytes 5906432 | tf_op jit(solution)/shard_map/while/body/eval_jaxpr/qhd,khd->hqk/dot_general | solution.py:61
  206.9 2.4 copy.43
  209.3 4.8 %fusion.54 = f32[128,16,80]{0,2,1:T(8,128)} fusion(bf16[512,16,80]{0,2,1:T(8,128)(2,1)} %bitcast.65, f32[16,512,128]{2,1,0:T(8,128)} %get-tuple-element.395, f32[16,128]{1,0:T(8,128)S(1)} %get-tuple-element.425, pred[128,512]{0,1:T(8,128)(4,1)S(1)} %broadcast_compare_fusion.2, f32[128,16,80]{0,2,1:T(8,128)} %get-tuple-element.414, ...), kind=kOutput, calls=%fused_computation.8.clone.1 | convolution fusion | flops 173506560 | bytes 6897665 | tf_op jit(solution)/shard_map/while/body/eval_jaxpr/hqk,khd->qhd/dot_general | solution.py:75
  215.3 3.5 %constant_dynamic-slice_fusion.3 = (bf16[512,1280]{1,0:T(8,128)(2,1)}, bf16[512,1280]{1,0:T(8,128)(2,1)}) fusion(bf16[1024,1280]{1,0:T(8,128)(2,1)} %get-tuple-element.432, s32[]{:T(128)S(6)} %select_n.85, bf16[1024,1280]{1,0:T(8,128)(2,1)} %get-tuple-element.430), kind=kLoop, calls=%fused_computation.19.clone.1 | loop fusion | bytes 5242884 | tf_op jit(solution)/shard_map/while/body/eval_jaxpr/dynamic_slice | solution.py:148
  218.7 2.4 copy.42
  221.4 4.3 %fusion.50 = (f32[16,128]{1,0:T(8,128)S(1)}, f32[16,512,128]{2,1,0:T(8,128)}) fusion(pred[128,512]{0,1:T(8,128)(4,1)S(1)} %broadcast_compare_fusion.2, bf16[512,16,80]{0,2,1:T(8,128)(2,1)} %bitcast.64, bf16[128,16,80]{0,2,1:T(8,128)(2,1)S(1)} %get-tuple-element.431), kind=kOutput, calls=%fused_computation.2.clone.1 | convolution fusion | flops 170915840 | bytes 5906432 | tf_op jit(solution)/shard_map/while/body/eval_jaxpr/qhd,khd->hqk/dot_general | solution.py:61
  225.7 2.4 copy.43
  228.1 5.0 %fusion.54 = f32[128,16,80]{0,2,1:T(8,128)} fusion(bf16[512,16,80]{0,2,1:T(8,128)(2,1)} %bitcast.65, f32[16,512,128]{2,1,0:T(8,128)} %get-tuple-element.395, f32[16,128]{1,0:T(8,128)S(1)} %get-tuple-element.425, pred[128,512]{0,1:T(8,128)(4,1)S(1)} %broadcast_compare_fusion.2, f32[128,16,80]{0,2,1:T(8,128)} %get-tuple-element.414, ...), kind=kOutput, calls=%fused_computation.8.clone.1 | convolution fusion | flops 173506560 | bytes 6897665 | tf_op jit(solution)/shard_map/while/body/eval_jaxpr/hqk,khd->qhd/dot_general | solution.py:75
  234.2 1.1 divide_convert_fusion
  235.3 45.3 %all-gather.11.cloned.1.call-done = bf16[1280,1280]{1,0:T(8,128)(2,1)} async-done(((bf16[40,1280]{1,0:T(8,128)(2,1)}), bf16[1280,1280]{1,0:T(8,128)(2,1)}) %all-gather.11.cloned.1.call-update) | async-done | bytes 3276816 | tf_op jit(solution)/shard_map/all_gather | solution.py:163
  280.7 3.4 %fusion.18 = bf16[128,1280]{1,0:T(8,128)(2,1)} fusion(f32[128,1280]{1,0:T(8,128)} %copy-done.2, bf16[128,1280]{0,1:T(8,128)(2,1)S(1)} %bitcast.72, bf16[1280,1280]{1,0:T(8,128)(2,1)} %all-gather.11.cloned.1.call-done, f32[1280]{0:T(1024)S(1)} %copy-done.8), kind=kOutput, calls=%fused_computation.27 | convolution fusion | flops 419921920 | bytes 4592640 | tf_op jit(solution)/shard_map/dot_general | solution.py:161
  (63 shorter events, 11.6 us)
Async XLA Ops:
  6.5 29.0 %copy-start = (bf16[1176,1280]{1,0:T(8,128)(2,1)S(1)}, bf16[1176,1280]{1,0:T(8,128)(2,1)}, u32[]{:S(2)}) copy-start(bf16[1176,1280]{1,0:T(8,128)(2,1)} %param.13) | copy-start | bytes 9031684
  6.5 111.7 %all-gather.5.cloned.1.call-start = ((), (), s32[]{:S(2)}) async-start(), calls=%async_computation.1 | async-start | bytes 10137600 | tf_op jit(solution)/shard_map/all_gather | solution.py:109
  9.4 25.0 %all-to-all-start = ((bf16[32,4,1176]{2,1,0:T(4,128)(2,1)}), bf16[32,4,1176]{2,1,0:T(4,128)(2,1)}, u32[]{:S(2)}, u32[]{:S(2)}) async-start(bf16[32,4,1176]{2,1,0:T(4,128)(2,1)} %all_to_all.8), calls=%async_computation | async-start | bytes 655360 | tf_op jit(solution)/shard_map/all_to_all | solution.py:97
  20.8 144.5 %all-gather.7.cloned.1.call-start = ((), (), s32[]{:S(2)}) async-start(), calls=%async_computation.2 | async-start | bytes 2949120 | tf_op jit(solution)/shard_map/all_gather | solution.py:140
  23.7 94.6 %copy-start.4 = (f32[1280]{0:T(1024)S(1)}, f32[1280]{0:T(1024)}, u32[]{:S(2)}) copy-start(f32[1280]{0:T(1024)} %param.15) | copy-start | bytes 15364
  23.7 94.6 %copy-start.5 = (f32[1280]{0:T(1024)S(1)}, f32[1280]{0:T(1024)}, u32[]{:S(2)}) copy-start(f32[1280]{0:T(1024)} %param.14) | copy-start | bytes 15364
  23.7 94.6 %copy-start.7 = (f32[3840]{0:T(1024)S(1)}, f32[3840]{0:T(1024)}, u32[]{:S(2)}) copy-start(f32[3840]{0:T(1024)} %param.17) | copy-start | bytes 46084
  36.2 0.9 copy-start.2
  123.8 1.3 copy-start.3
  137.4 59.1 %copy-start.6 = (s32[1,3]{1,0:T(1,128)S(1)}, s32[1,3]{1,0:T(1,128)}, u32[]{:S(2)}) copy-start(s32[1,3]{1,0:T(1,128)} %param.20) | copy-start | bytes 40
  140.3 56.1 %all-gather.9.cloned.1.call-start = ((), (), s32[]{:S(2)}) async-start(), calls=%async_computation.3 | async-start | bytes 2949120 | tf_op jit(solution)/shard_map/all_gather | solution.py:141
  142.2 138.4 %all-gather.11.cloned.1.call-start = ((), (), s32[]{:S(2)}) async-start(), calls=%async_computation.4 | async-start | bytes 3379200 | tf_op jit(solution)/shard_map/all_gather | solution.py:163
  196.5 84.2 %copy-start.8 = (f32[1280]{0:T(1024)S(1)}, f32[1280]{0:T(1024)}, u32[]{:S(2)}) copy-start(f32[1280]{0:T(1024)} %param.19) | copy-start | bytes 15364
  209.3 4.9 %copy-start.1 = (f32[16,512,128]{2,1,0:T(8,128)S(1)}, f32[16,512,128]{2,1,0:T(8,128)}, u32[]{:S(2)}) copy-start(f32[16,512,128]{2,1,0:T(8,128)} %get-tuple-element.395) | copy-start | bytes 12582916 | tf_op jit(solution)/shard_map/while
  228.1 5.0 %copy-start.1 = (f32[16,512,128]{2,1,0:T(8,128)S(1)}, f32[16,512,128]{2,1,0:T(8,128)}, u32[]{:S(2)}) copy-start(f32[16,512,128]{2,1,0:T(8,128)} %get-tuple-element.395) | copy-start | bytes 12582916 | tf_op jit(solution)/shard_map/while
Sparse Core Ops, SparseCore 0:
  10.0 108.2 all-gather.4
  140.4 24.8 all-gather.6
  167.2 29.2 all-gather.8
  198.9 81.7 all-gather.10
where the time goes:
time: 291 us
  waiting for transfers between devices  188 us (65%)
  local copies, waits for them, and re-layouts  38 us (13%)
  matrix products  28.1 us (10%)
  between operations  13.3 us (5%)
  starting transfers between devices  11.6 us (4%)
  other arithmetic  11.2 us (4%)
    all_gather x1, waiting for transfers between devices, per_device(): lax.all_gather(qkv_weight, 'dp', axis=0, tiled=True)  81 us
    all_gather x1, waiting for transfers between devices, per_device(): lax.all_gather(out_weight, 'dp', axis=0, tiled=True)  45.3 us
    all_gather x1, waiting for transfers between devices, per_device(): piece_values = lax.all_gather(values, 'seq', axis=0, tiled=True)  31.1 us
    all_gather x1, waiting for transfers between devices, per_device(): piece_keys = lax.all_gather(key_rows, 'seq', axis=0, tiled=True)  21.3 us
    dynamic_slice x4, local copies, waits for them, and re-layouts, one_block(): value_block = lax.dynamic_slice_in_dim(piece_values, first_row, length, 0)  11.8 us
    all_to_all x1, starting transfers between devices, per_device(): lax.all_to_all(pixels, 'dp', split_axis=0, concat_axis=0, tiled=True)  11.4 us
    dot_general x2, matrix products, attend_block(): jnp.einsum('hqk,khd->qhd', weights.astype(jnp.bfloat16), value_block.resh...  9.84 us
    dot_general x2, matrix products, attend_block(): jnp.einsum('qhd,khd->hqk', queries3, key_block.reshape(count, HEADS, HDIM...  8.54 us
  transfers between devices with their start and end apart: 5, of which 5 were waited for; matrix products, arithmetic and copies ran while one was open for 17% of the time, Pallas kernels for 0%

commit v1 on v0

--- a/solution.py
+++ b/solution.py
@@ -1,3 +1,4 @@
+import functools
 import jax
 import jax.numpy as jnp
 from jax import lax
@@ -5,6 +6,18 @@
 
 HEADS = 16
 HDIM = 80
+
+
+def quarters_play(original, mesh_dim, array_dim):
+    return jnp.concatenate(
+        lax.all_to_all(
+            jnp.stack([original for _ in range(lax.axis_size(mesh_dim))], 0), mesh_dim, 0, 0
+        ),
+        array_dim,
+    )
+
+
+edit_bands_over_axis = functools.partial(quarters_play, mesh_dim="dp", array_dim=0)
 
 
 def image_lookup(positions, starts):
@@ -104,11 +117,7 @@
     normed = layer_norm(embedded, ln_gain, ln_bias)
     columns = normed
     projected = (
-        jnp.dot(
-            columns,
-            lax.all_gather(qkv_weight, "dp", axis=0, tiled=True),
-            preferred_element_type=jnp.float32,
-        )
+        jnp.dot(columns, edit_bands_over_axis(qkv_weight), preferred_element_type=jnp.float32)
         + qkv_bias
     )
     starts = offsets[0]

time: 291 us -> 446 us (1.53)
  waiting for transfers between devices: 188 us -> 319 us
  blocking collectives: 0 us -> 24.8 us
  starting transfers between devices: 11.6 us -> 5.24 us
  local copies, waits for them, and re-layouts: 38 us -> 44.2 us
    all_to_all x1, waiting for transfers between devices: 8.46 us -> 212 us  [quarters_play(): lax.all_to_all(jnp.stack([original for _ in range(lax.axis_size(mesh_dim)...]
    all_gather x1 -> x0, waiting for transfers between devices: 81 us -> none  [per_device(): lax.all_gather(qkv_weight, 'dp', axis=0, tiled=True)]
    all_to_all x0 -> x1, blocking collectives: none -> 24.8 us  [per_device(): lax.all_to_all(pixels, 'dp', split_axis=0, concat_axis=0, tiled=True)]
    all_gather x1, waiting for transfers between devices: 21.3 us -> 29.7 us  [per_device(): piece_keys = lax.all_gather(key_rows, 'seq', axis=0, tiled=True)]
    all_to_all x1, starting transfers between devices: 11.4 us -> 5.11 us  [quarters_play(): lax.all_to_all(jnp.stack([original for _ in range(lax.axis_size(mesh_dim)...]
    another operation x0 -> x1, local copies, waits for them, and re-layouts: none -> 5.37 us  [quarters_play(): jnp.stack([original for _ in range(lax.axis_size(mesh_dim))], 0)]
  transfers between devices with their start and end apart: 5 -> 4, of which waited for: 5 -> 4; matrix products, arithmetic and copies ran while one was open for 17% -> 10% of each run, Pallas kernels for 0% -> 0%
where the time goes in v1:
time: 446 us; the launch traced here: 445 us
  waiting for transfers between devices  319 us (72%)
  local copies, waits for them, and re-layouts  44.2 us (10%)
  matrix products  28.1 us (6%)
  blocking collectives  24.8 us (6%)
  between operations  13.3 us (3%)
  other arithmetic  9.9 us (2%)
  starting transfers between devices  5.24 us (1%)
    all_to_all x1, waiting for transfers between devices, quarters_play(): lax.all_to_all(jnp.stack([original for _ in range(lax.axis_size(mesh_dim)...  212 us
    all_gather x1, waiting for transfers between devices, per_device(): lax.all_gather(out_weight, 'dp', axis=0, tiled=True)  45.5 us
    all_gather x1, waiting for transfers between devices, per_device(): piece_values = lax.all_gather(values, 'seq', axis=0, tiled=True)  31.1 us
    all_gather x1, waiting for transfers between devices, per_device(): piece_keys = lax.all_gather(key_rows, 'seq', axis=0, tiled=True)  29.7 us
    all_to_all x1, blocking collectives, per_device(): lax.all_to_all(pixels, 'dp', split_axis=0, concat_axis=0, tiled=True)  24.8 us
    dynamic_slice x4, local copies, waits for them, and re-layouts, one_block(): value_block = lax.dynamic_slice_in_dim(piece_values, first_row, length, 0)  11.8 us
    dot_general x2, matrix products, attend_block(): jnp.einsum('hqk,khd->qhd', weights.astype(jnp.bfloat16), value_block.resh...  9.86 us
  transfers between devices with their start and end apart: 4, of which 4 were waited for; matrix products, arithmetic and copies ran while one was open for 10% of the time, Pallas kernels for 0%

profile of v1, /device:TPU:8, one launch (start us, length us, event | category | flops | bytes accessed | tf_op | source)
XLA Modules:
  0.0 444.7 jit_solution(385462956212304883)
XLA Ops:
  6.5 2.0 copy.27
  9.6 24.8 %all_to_all.17 = bf16[32,4,1176]{2,1,0:T(4,128)(2,1)} all-to-all(bf16[32,4,1176]{2,1,0:T(4,128)(2,1)S(1)} %all_to_all.11), channel_id=1, replica_groups=mesh['dp'=32,'seq'=8] {'dp'}, dimensions={0} | all-to-all | bytes 602112 | tf_op jit(solution)/shard_map/all_to_all | solution.py:110
  34.4 5.4 %stack.2 = bf16[32,40,3840]{2,1,0:T(8,128)(2,1)} broadcast(bf16[40,3840]{1,0:T(8,128)(2,1)} %param.16), dimensions={1,2} | broadcast | bytes 10137600 | tf_op jit(solution)/shard_map/stack | solution.py:14
  39.8 5.1 %all-to-all-start.1 = ((bf16[32,40,3840]{2,1,0:T(8,128)(2,1)}), bf16[32,40,3840]{2,1,0:T(8,128)(2,1)}, u32[]{:S(2)}, u32[]{:S(2)}) async-start(bf16[32,40,3840]{2,1,0:T(8,128)(2,1)} %stack.2), calls=%async_computation.1 | async-start | bytes 19660800 | tf_op jit(solution)/shard_map/all_to_all | solution.py:13
  46.5 2.2 copy.28
  51.5 212.1 %all-to-all-done.1 = bf16[32,40,3840]{2,1,0:T(8,128)(2,1)} async-done(((bf16[32,40,3840]{2,1,0:T(8,128)(2,1)}), bf16[32,40,3840]{2,1,0:T(8,128)(2,1)}, u32[]{:S(2)}, u32[]{:S(2)}) %all-to-all-start.1) | async-done | bytes 9830432 | tf_op jit(solution)/shard_map/all_to_all | solution.py:13
  263.6 5.5 %convolution_add_fusion = f32[128,3840]{1,0:T(8,128)S(1)} fusion(bf16[1280,3840]{1,0:T(8,128)(2,1)} %bitcast.1, f32[3840]{0:T(1024)S(1)} %copy-done.7, f32[128,1280]{1,0:T(8,128)} %copy-done.2, f32[1280]{0:T(1024)S(1)} %copy-done.4, f32[1280]{0:T(1024)S(1)} %copy-done.5, f32[128]{0:T(128)S(1)} %add_rsqrt_fusion, f32[128]{0:T(128)S(1)} %broadcast_multiply_fusion.2), kind=kOutput, calls=%fused_computation.24 | convolution fusion | flops 1259601920 | bytes 12478464 | tf_op jit(solution)/shard_map/dot_general | solution.py:120
  269.2 1.3 copy-done.3
  270.5 1.2 fusion.27
  271.6 2.2 copy.29
  273.8 2.2 copy.32
  276.0 1.4 slice_negate_fusion
  278.5 2.2 copy.30
  280.6 2.2 copy.33
  282.8 2.9 add_convert_fusion
  285.8 1.9 slice.41
  288.4 1.2 copy.34
  289.6 29.7 %all-gather.4.cloned.1.call-done = bf16[1024,1280]{1,0:T(8,128)(2,1)} async-done(((bf16[128,1280]{1,0:T(8,128)(2,1)}), bf16[1024,1280]{1,0:T(8,128)(2,1)}) %all-gather.4.cloned.1.call-update) | async-done | bytes 2621456 | tf_op jit(solution)/shard_map/all_gather | solution.py:149
  319.2 31.1 %all-gather.6.cloned.1.call-done = bf16[1024,1280]{1,0:T(8,128)(2,1)} async-done(((bf16[128,1280]{1,0:T(8,128)(2,1)}), bf16[1024,1280]{1,0:T(8,128)(2,1)}) %all-gather.6.cloned.1.call-update) | async-done | bytes 2621456 | tf_op jit(solution)/shard_map/all_gather | solution.py:150
  350.4 37.7 %while.20 = (s32[]{:T(128)}, f32[16,128]{1,0:T(8,128)S(1)}, f32[16,128]{1,0:T(8,128)S(1)}, f32[128,16,80]{0,2,1:T(8,128)}, s32[128]{0:T(128)S(1)}, /*index=5*/s3...) while((s32[]{:T(128)}, f32[16,128]{1,0:T(8,128)S(1)}, ...), condition=%wide.region_9.10_spmd.clone, body=%wide.region_5.9_spmd.clone.sunk | while | flops 349750272 | bytes 44511972 | solution.py:163
  350.4 3.5 constant_dynamic-slice_fusion.3
  353.8 2.4 copy.42
  356.5 4.3 fusion.50
  360.8 2.4 copy.43
  363.2 4.9 %fusion.54 = f32[128,16,80]{0,2,1:T(8,128)} fusion(bf16[512,16,80]{0,2,1:T(8,128)(2,1)} %bitcast.66, f32[16,512,128]{2,1,0:T(8,128)} %get-tuple-element.395, f32[16,128]{1,0:T(8,128)S(1)} %get-tuple-element.425, pred[128,512]{0,1:T(8,128)(4,1)S(1)} %broadcast_compare_fusion.2, f32[128,16,80]{0,2,1:T(8,128)} %get-tuple-element.414, ...), kind=kOutput, calls=%fused_computation.8.clone.1 | convolution fusion | flops 173506560 | bytes 6897665 | tf_op jit(solution)/shard_map/while/body/eval_jaxpr/hqk,khd->qhd/dot_general | solution.py:88
  369.1 3.5 constant_dynamic-slice_fusion.3
  372.6 2.4 copy.42
  375.3 4.3 fusion.50
  379.6 2.4 copy.43
  382.0 5.0 %fusion.54 = f32[128,16,80]{0,2,1:T(8,128)} fusion(bf16[512,16,80]{0,2,1:T(8,128)(2,1)} %bitcast.66, f32[16,512,128]{2,1,0:T(8,128)} %get-tuple-element.395, f32[16,128]{1,0:T(8,128)S(1)} %get-tuple-element.425, pred[128,512]{0,1:T(8,128)(4,1)S(1)} %broadcast_compare_fusion.2, f32[128,16,80]{0,2,1:T(8,128)} %get-tuple-element.414, ...), kind=kOutput, calls=%fused_computation.8.clone.1 | convolution fusion | flops 173506560 | bytes 6897665 | tf_op jit(solution)/shard_map/while/body/eval_jaxpr/hqk,khd->qhd/dot_general | solution.py:88
  389.2 45.5 %all-gather.8.cloned.1.call-done = bf16[1280,1280]{1,0:T(8,128)(2,1)} async-done(((bf16[40,1280]{1,0:T(8,128)(2,1)}), bf16[1280,1280]{1,0:T(8,128)(2,1)}) %all-gather.8.cloned.1.call-update) | async-done | bytes 3276816 | tf_op jit(solution)/shard_map/all_gather | solution.py:172
  434.7 3.4 fusion.18
  (64 shorter events, 11.1 us)
Async XLA Ops:
  6.5 43.2 %copy-start = (bf16[1176,1280]{1,0:T(8,128)(2,1)S(1)}, bf16[1176,1280]{1,0:T(8,128)(2,1)}, u32[]{:S(2)}) copy-start(bf16[1176,1280]{1,0:T(8,128)(2,1)} %param.13) | copy-start | bytes 9031684
  39.8 5.2 %copy-start.6 = (s32[1,3]{1,0:T(1,128)S(1)}, s32[1,3]{1,0:T(1,128)}, u32[]{:S(2)}) copy-start(s32[1,3]{1,0:T(1,128)} %param.20) | copy-start | bytes 40
  39.8 5.3 %copy-start.9 = (s32[1,3]{1,0:T(1,128)S(1)}, s32[1,3]{1,0:T(1,128)}, u32[]{:S(2)}) copy-start(s32[1,3]{1,0:T(1,128)} %param.21) | copy-start | bytes 40
  39.8 223.8 %all-to-all-start.1 = ((bf16[32,40,3840]{2,1,0:T(8,128)(2,1)}), bf16[32,40,3840]{2,1,0:T(8,128)(2,1)}, u32[]{:S(2)}, u32[]{:S(2)}) async-start(bf16[32,40,3840]{2,1,0:T(8,128)(2,1)} %stack.2), calls=%async_computation.1 | async-start | bytes 19660800 | tf_op jit(solution)/shard_map/all_to_all | solution.py:13
  44.9 218.7 %copy-start.4 = (f32[1280]{0:T(1024)S(1)}, f32[1280]{0:T(1024)}, u32[]{:S(2)}) copy-start(f32[1280]{0:T(1024)} %param.15) | copy-start | bytes 15364
  44.9 218.7 %copy-start.5 = (f32[1280]{0:T(1024)S(1)}, f32[1280]{0:T(1024)}, u32[]{:S(2)}) copy-start(f32[1280]{0:T(1024)} %param.14) | copy-start | bytes 15364
  44.9 218.7 %copy-start.7 = (f32[3840]{0:T(1024)S(1)}, f32[3840]{0:T(1024)}, u32[]{:S(2)}) copy-start(f32[3840]{0:T(1024)} %param.17) | copy-start | bytes 46084
  44.9 274.3 %all-gather.4.cloned.1.call-start = ((), (), s32[]{:S(2)}) async-start(), calls=%async_computation.2 | async-start | bytes 2949120 | tf_op jit(solution)/shard_map/all_gather | solution.py:149
  50.4 0.8 copy-start.2
  269.2 1.3 copy-start.3
  285.7 64.7 %all-gather.6.cloned.1.call-start = ((), (), s32[]{:S(2)}) async-start(), calls=%async_computation.3 | async-start | bytes 2949120 | tf_op jit(solution)/shard_map/all_gather | solution.py:150
  287.6 147.1 %all-gather.8.cloned.1.call-start = ((), (), s32[]{:S(2)}) async-start(), calls=%async_computation.4 | async-start | bytes 3379200 | tf_op jit(solution)/shard_map/all_gather | solution.py:172
  350.4 84.4 %copy-start.8 = (f32[1280]{0:T(1024)S(1)}, f32[1280]{0:T(1024)}, u32[]{:S(2)}) copy-start(f32[1280]{0:T(1024)} %param.19) | copy-start | bytes 15364
  363.2 4.9 %copy-start.1 = (f32[16,512,128]{2,1,0:T(8,128)S(1)}, f32[16,512,128]{2,1,0:T(8,128)}, u32[]{:S(2)}) copy-start(f32[16,512,128]{2,1,0:T(8,128)} %get-tuple-element.395) | copy-start | bytes 12582916 | tf_op jit(solution)/shard_map/while
  382.0 5.0 %copy-start.1 = (f32[16,512,128]{2,1,0:T(8,128)S(1)}, f32[16,512,128]{2,1,0:T(8,128)}, u32[]{:S(2)}) copy-start(f32[16,512,128]{2,1,0:T(8,128)} %get-tuple-element.395) | copy-start | bytes 12582916 | tf_op jit(solution)/shard_map/while
Sparse Core Ops, SparseCore 0:
  285.8 33.3 all-gather.3
  321.1 29.2 all-gather.5
  353.0 81.7 all-gather.7
